TPU v7x, 32 devices: a whole 2x2x4 slice. The times are simulated.
32 devices in a mesh: grp: 2 (over x), feat: 8 (over z, y), tok: 2 (over core).
Axes of the slice: x: 2, y: 2, z: 4, core: 2. Of those that a mesh axis runs over, the one named last changes fastest.
Arguments:
- tokens: bfloat16 [2048, 8192], P(('grp', 'tok'), 'feat'), parts along dimension 0, may hold values from -6 to 6
- in_weight: bfloat16 [8192, 3, 8192], P('tok', None, 'feat'), may hold values from -0.0625 to 0.0625
- filters: float32 [512, 128], P('feat'), may hold values from -0.5 to 0.5
- out_weight: bfloat16 [8192, 8192], P('feat'), may hold values from -0.09375 to 0.09375
Outputs:
- mixed_out: bfloat16 [2048, 8192], P(('grp', 'tok'), 'feat'), parts along dimension 0
There are 2 independent parts, one for each index of `grp`. A program takes and returns all parts, laid end to end along the dimension named above; an argument that names none is the same for every part. Nothing has to cross between parts.
All inputs are finite; a program needn't handle non-finite values.
Results may differ from a plain program's by a relative error of at most 0.024.
Values may be sent and summed in bfloat16 or wider, within the bound.
A program may use at most 192 MiB of HBM per device.

v0:
```python
import jax
import jax.numpy as jnp
from jax import lax
from jax.sharding import PartitionSpec as P

GROUP = 16


def shifted(block, axis, distance):
    devices = range(lax.axis_size(axis))
    route = [(i - distance, i) for i in devices if i - distance in devices]
    return lax.ppermute(block, axis, route)


def shards(tokens, in_weight, filters, out_weight):
    rows = tokens.shape[0]
    panel = lax.all_gather(in_weight, "tok", axis=0, tiled=True)
    channels = panel.shape[2]
    flat_panel = panel.reshape(panel.shape[0], 3 * channels)
    proj = jnp.dot(
        lax.all_gather(tokens, "feat", axis=1, tiled=True),
        flat_panel,
        preferred_element_type=jnp.float32,
    ).astype(jnp.bfloat16)
    query = proj[:, :channels].astype(jnp.float32)
    gated = (
        proj[:, channels : 2 * channels].astype(jnp.float32)
        * proj[:, 2 * channels :].astype(jnp.float32)
    ).astype(jnp.bfloat16)
    halo = filters.shape[1] - 1
    earlier = shifted(gated[rows - halo :], "tok", 1)
    extended = jnp.concatenate([earlier, gated], axis=0).astype(jnp.float32)
    taps = jnp.broadcast_to(filters[:, None, :], (filters.shape[0], GROUP, filters.shape[1]))
    taps = taps.reshape(channels, filters.shape[1]).T

    def add_tap(j, total):
        window = lax.dynamic_slice_in_dim(extended, halo - j, rows, 0)
        coeff = lax.dynamic_index_in_dim(taps, j, 0, keepdims=True)
        return total + window * coeff

    conv = lax.fori_loop(0, filters.shape[1], add_tap, jnp.zeros((rows, channels), jnp.float32))
    hidden = (query * conv).astype(jnp.bfloat16)
    partial_rows = jnp.dot(hidden, out_weight, preferred_element_type=jnp.float32)
    result = lax.psum_scatter(
        partial_rows.astype(jnp.bfloat16), "feat", scatter_dimension=1, tiled=True
    )
    return result


def solution(mesh):
    in_specs = (P(("grp", "tok"), "feat"), P("tok", None, "feat"), P("feat", None), P("feat", None))
    out_specs = P(("grp", "tok"), "feat")
    return jax.shard_map(shards, mesh=mesh, in_specs=in_specs, out_specs=out_specs, check_vma=False)
```

profile of v0, /device:TPU:0, one launch (start us, length us, event | category | flops | bytes accessed | tf_op | source)
XLA Modules:
  0.0 874.1 jit_solution(4274934379387335088)
XLA Ops:
  7.3 33.5 %copy.6 = bf16[4096,3,1024]{0,2,1:T(8,128)(2,1)} copy(bf16[4096,3,1024]{2,0,1:T(8,128)(2,1)} %param.7) | data formatting | bytes 50331648 | tf_op args[1]
  40.9 96.3 %all-gather.3.cloned.1.call-done = bf16[512,8192]{1,0:T(8,128)(2,1)} async-done(((bf16[512,1024]{1,0:T(8,128)(2,1)}), bf16[512,8192]{1,0:T(8,128)(2,1)}) %all-gather.3.cloned.1.call-update) | async-done | bytes 8388624 | tf_op jit(solution)/shard_map/all_gather | solution.py:21
  137.2 72.9 %all-gather.5.cloned.1.call-done = bf16[8192,3,1024]{0,2,1:T(8,128)(2,1)} async-done(((bf16[4096,3,1024]{0,2,1:T(8,128)(2,1)}), bf16[8192,3,1024]{0,2,1:T(8,128)(2,1)}) %all-gather.5.cloned.1.call-update) | async-done | bytes 50331664 | tf_op jit(solution)/shard_map/all_gather | solution.py:17
  210.1 33.0 %convolution_convert_fusion.1 = bf16[512,3072]{1,0:T(8,128)(2,1)S(1)} fusion(bf16[512,8192]{1,0:T(8,128)(2,1)} %all-gather.3.cloned.1.call-done, bf16[8192,3072]{0,1:T(8,128)(2,1)} %bitcast.12), kind=kOutput, calls=%fused_computation.3 | convolution fusion | flops 25771376640 | bytes 61865984 | tf_op jit(solution)/shard_map/dot_general | solution.py:20
  249.9 449.5 %while.16 = (s32[]{:T(128)}, f32[512,1024]{1,0:T(8,128)}, f32[639,1024]{1,0:T(8,128)S(1)}, f32[128,1024]{1,0:T(8,128)S(1)}, s32[]{:T(128)}, /*index=5*/s32[]{:T(128)}, s32[]{:T(128)}, s32[]{:T(128)}) while((s32[]{:T(128)}, f32[512,1024]{1,0:T(8,128)}, f32[639,1024]{1,0:T(8,128)S(1)}, f32[128,1024]{1,0:T(8,128)S(1)}, s32[]{:T(128)}, ...), condition=%wide.region_1.2_spmd.clone, body=%wide.region_0.1_spmd.clone.sunk | while | flops 1572871 | bytes 6303893 | solution.py:41
  251.9 3.5 select_add_fusion.2
  255.5 3.5 select_add_fusion.2
  259.0 3.5 select_add_fusion.2
  262.5 3.5 select_add_fusion.2
  266.0 3.5 select_add_fusion.2
  269.5 3.5 select_add_fusion.2
  273.1 3.5 select_add_fusion.2
  276.6 3.5 select_add_fusion.2
  280.1 3.5 select_add_fusion.2
  283.6 3.5 select_add_fusion.2
  287.2 3.5 select_add_fusion.2
  290.7 3.5 select_add_fusion.2
  294.2 3.5 select_add_fusion.2
  297.7 3.5 select_add_fusion.2
  301.3 3.5 select_add_fusion.2
  304.8 3.5 select_add_fusion.2
  308.3 3.5 select_add_fusion.2
  311.8 3.5 select_add_fusion.2
  315.4 3.5 select_add_fusion.2
  318.9 3.5 select_add_fusion.2
  322.4 3.5 select_add_fusion.2
  325.9 3.5 select_add_fusion.2
  329.5 3.5 select_add_fusion.2
  333.0 3.5 select_add_fusion.2
  336.5 3.5 select_add_fusion.2
  340.0 3.5 select_add_fusion.2
  343.5 3.5 select_add_fusion.2
  347.1 3.5 select_add_fusion.2
  350.6 3.5 select_add_fusion.2
  354.1 3.5 select_add_fusion.2
  357.6 3.5 select_add_fusion.2
  361.2 3.5 select_add_fusion.2
  364.7 3.5 select_add_fusion.2
  368.2 3.5 select_add_fusion.2
  371.7 3.5 select_add_fusion.2
  375.3 3.5 select_add_fusion.2
  378.8 3.5 select_add_fusion.2
  382.3 3.5 select_add_fusion.2
  385.8 3.5 select_add_fusion.2
  389.4 3.5 select_add_fusion.2
  392.9 3.5 select_add_fusion.2
  396.4 3.5 select_add_fusion.2
  399.9 3.5 select_add_fusion.2
  403.4 3.5 select_add_fusion.2
  417.5 3.5 select_add_fusion.2
  435.2 3.5 select_add_fusion.2
  466.9 3.5 select_add_fusion.2
  484.5 3.5 select_add_fusion.2
  502.1 3.5 select_add_fusion.2
  533.8 3.5 select_add_fusion.2
  551.4 3.5 select_add_fusion.2
  569.1 3.5 select_add_fusion.2
  600.8 3.5 select_add_fusion.2
  618.4 3.5 select_add_fusion.2
  636.0 3.5 select_add_fusion.2
  667.7 3.5 select_add_fusion.2
  685.3 3.5 select_add_fusion.2
  699.4 17.3 %convolution_convert_fusion = bf16[512,8192]{1,0:T(8,128)(2,1)} fusion(bf16[1024,8192]{1,0:T(8,128)(2,1)} %param.9, f32[512,1024]{1,0:T(8,128)} %get-tuple-element.115, bf16[512,3072]{1,0:T(8,128)(2,1)} %copy-done.1), kind=kOutput, calls=%fused_computation.2 | convolution fusion | flops 8595701760 | bytes 28311552 | tf_op jit(solution)/shard_map/dot_general | solution.py:43
  716.7 150.9 %reduce-scatter.2.cloned.1.call-done = bf16[512,1024]{1,0:T(8,128)(2,1)} async-done(((bf16[512,8192]{1,0:T(8,128)(2,1)}), bf16[512,1024]{1,0:T(8,128)(2,1)}) %reduce-scatter.2.cloned.1.call-update) | async-done | bytes 1048592 | tf_op jit(solution)/shard_map/reduce_scatter | solution.py:44
  (219 shorter events, 256.5 us)
Async XLA Ops:
  6.5 130.7 %all-gather.3.cloned.1.call-start = ((), (), s32[]{:S(2)}) async-start(), calls=%async_computation.1 | async-start | bytes 9437184 | tf_op jit(solution)/shard_map/all_gather | solution.py:21
  7.3 202.9 %all-gather.5.cloned.1.call-start = ((), (), s32[]{:S(2)}) async-start(), calls=%async_computation.2 | async-start | bytes 75497472 | tf_op jit(solution)/shard_map/all_gather | solution.py:17
  40.9 826.7 %reduce-scatter.2.cloned.1.call-start = ((), (), s32[]{:S(2)}) async-start(), calls=%async_computation.3 | async-start | bytes 9437184 | tf_op jit(solution)/shard_map/reduce_scatter | solution.py:44
  243.1 2.0 copy-start.1
  243.1 4.1 copy-start.2
  243.5 1.3 copy-start
  245.1 3.3 collective-permute-start
Sparse Core Ops, SparseCore 0:
  9.5 127.6 all-gather.2
  138.7 71.3 all-gather.4
  716.8 150.6 reduce-scatter.1
where the time goes:
time: 879 us; the launch traced here: 874 us
  other arithmetic  450 us (51%)
  waiting for transfers between devices  322 us (37%)
  matrix products  50.2 us (6%)
  local copies, waits for them, and re-layouts  36.3 us (4%)
  between operations  13.2 us (2%)
    add x128, other arithmetic, add_tap(): return total + window * coeff  448 us
    reduce_scatter x1, waiting for transfers between devices, shards(): lax.psum_scatter(partial_rows.astype(jnp.bfloat16), 'feat', scatter_dimen...  151 us
    all_gather x1, waiting for transfers between devices, shards(): lax.all_gather(tokens, 'feat', axis=1, tiled=True)  96.3 us
    all_gather x1, waiting for transfers between devices, shards(): panel = lax.all_gather(in_weight, 'tok', axis=0, tiled=True)  72.9 us
    unnamed x8, local copies, waits for them, and re-layouts  35.2 us
    dot_general x1, matrix products, shards(): jnp.dot(lax.all_gather(tokens, 'feat', axis=1, tiled=True), flat_panel, p...  33 us
  transfers between devices with their start and end apart: 4, of which 4 were waited for; matrix products, arithmetic and copies ran while one was open for 4% of the time, Pallas kernels for 0%

commit v1 on v0

v1 whole, which is shorter than its diff:
```python
import functools

import jax
import jax.numpy as jnp
from jax import lax
from jax.experimental import pallas as pl
from jax.experimental.pallas import tpu as pltpu
from jax.sharding import PartitionSpec as P

GROUP = 16
LANES = 128


def conv_kernel(band_ref, q_ref, k_ref, v_ref, out_ref):
    taps = band_ref.shape[2] // 2
    rows = q_ref.shape[0]
    blocks = rows // taps
    gated = (k_ref[...].astype(jnp.float32) * v_ref[...].astype(jnp.float32)).astype(jnp.bfloat16)
    right = jnp.concatenate(
        [gated[b * taps : (b + 2) * taps] for b in range(blocks)], axis=1
    )
    lane = lax.broadcasted_iota(jnp.int32, (taps, LANES), 1) // GROUP
    lane = jnp.concatenate([lane] * blocks, axis=1)
    total = jnp.zeros((taps, blocks * LANES), jnp.float32)
    for f in range(LANES // GROUP):
        row = jnp.broadcast_to(band_ref[0, f : f + 1, :], (taps, 2 * taps))
        band = pltpu.roll(row, 0, 1, stride=1, stride_axis=0).astype(jnp.bfloat16)
        product = jnp.dot(band, right, preferred_element_type=jnp.float32)
        total = jnp.where(lane == f, product, total)
    for b in range(blocks):
        at = slice(b * taps, (b + 1) * taps)
        out_ref[at, :] = (
            q_ref[at, :].astype(jnp.float32) * total[:, b * LANES : (b + 1) * LANES]
        ).astype(jnp.bfloat16)


def convolve(filters, query, keyed, valued):
    rows, channels = query.shape
    count, taps = filters.shape
    per = LANES // GROUP
    band = jnp.concatenate(
        [jnp.zeros((count, 1), jnp.float32), filters[:, ::-1], jnp.zeros((count, taps - 1), jnp.float32)],
        axis=1,
    ).reshape(count // per, per, 2 * taps)
    return pl.pallas_call(
        conv_kernel,
        grid=(channels // LANES,),
        out_shape=jax.ShapeDtypeStruct((rows, channels), jnp.bfloat16),
        in_specs=[
            pl.BlockSpec((1, per, 2 * taps), lambda i: (i, 0, 0)),
            pl.BlockSpec((rows, LANES), lambda i: (0, i)),
            pl.BlockSpec((rows + taps, LANES), lambda i: (0, i)),
            pl.BlockSpec((rows + taps, LANES), lambda i: (0, i)),
        ],
        out_specs=pl.BlockSpec((rows, LANES), lambda i: (0, i)),
        compiler_params=pltpu.CompilerParams(vmem_limit_bytes=24 * 1024 * 1024),
    )(band, query, keyed, valued)


def swap(block):
    return lax.ppermute(block, "tok", [(0, 1), (1, 0)])


def shards(tokens, in_weight, filters, out_weight):
    rows = tokens.shape[0]
    depth = in_weight.shape[0]
    channels = in_weight.shape[2]
    taps = filters.shape[1]
    me = lax.axis_index("tok")
    panel = jnp.transpose(in_weight, (1, 0, 2))
    full = lax.all_gather(tokens, "feat", axis=1, tiled=True)
    mine = lax.dynamic_slice_in_dim(full, me * depth, depth, 1)
    theirs = swap(lax.dynamic_slice_in_dim(full, (1 - me) * depth, depth, 1))

    def project(x):
        return [jnp.dot(x, panel[s], preferred_element_type=jnp.float32) for s in range(3)]

    away = [swap(p.astype(jnp.bfloat16)) for p in project(theirs)]
    home = project(mine)
    q, k, v = [(a.astype(jnp.float32) + b).astype(jnp.bfloat16) for a, b in zip(away, home)]

    def extend(x):
        return jnp.concatenate([lax.ppermute(x[rows - taps :], "tok", [(0, 1)]), x], axis=0)

    hidden = convolve(filters, q, extend(k), extend(v))
    partial_rows = jnp.dot(hidden, out_weight, preferred_element_type=jnp.float32)
    return lax.psum_scatter(
        partial_rows.astype(jnp.bfloat16), "feat", scatter_dimension=1, tiled=True
    )


def solution(mesh):
    in_specs = (P(("grp", "tok"), "feat"), P("tok", None, "feat"), P("feat", None), P("feat", None))
    out_specs = P(("grp", "tok"), "feat")
    return jax.shard_map(shards, mesh=mesh, in_specs=in_specs, out_specs=out_specs, check_vma=False)
```

time: 879 us -> 376 us (0.43)
  other arithmetic: 450 us -> 1.41 us
  waiting for transfers between devices: 322 us -> 279 us
  local copies, waits for them, and re-layouts: 36.3 us -> 4.85 us
  matrix products: 50.2 us -> 66.6 us
    add x128 -> x0, other arithmetic: 448 us -> none  [add_tap(): return total + window * coeff]
    all_gather x2 -> x1, waiting for transfers between devices: 169 us -> 130 us  [shards(): full = lax.all_gather(tokens, 'feat', axis=1, tiled=True)]
    unnamed x8 -> x4, local copies, waits for them, and re-layouts: 35.2 us -> 0.01 us
    dot_general x1 -> x6, matrix products: 33 us -> 49.8 us  [project(): jnp.dot(x, panel[s], preferred_element_type=jnp.float32)]
  transfers between devices with their start and end apart: 4 -> 8, of which waited for: 4 -> 3; matrix products, arithmetic and copies ran while one was open for 4% -> 11% of each run, Pallas kernels for 0% -> 0%
where the time goes in v1:
time: 376 us; the launch traced here: 375 us
  waiting for transfers between devices  279 us (74%)
  matrix products  66.6 us (18%)
  between operations  13.6 us (4%)
  Pallas kernels  5.42 us (1%)
  local copies, waits for them, and re-layouts  4.85 us (1%)
  starting transfers between devices  4.73 us (1%)
    reduce_scatter x1, waiting for transfers between devices, shards(): lax.psum_scatter(partial_rows.astype(jnp.bfloat16), 'feat', scatter_dimen...  148 us
    all_gather x1, waiting for transfers between devices, shards(): full = lax.all_gather(tokens, 'feat', axis=1, tiled=True)  130 us
    dot_general x6, matrix products, project(): jnp.dot(x, panel[s], preferred_element_type=jnp.float32)  49.8 us
    dot_general x1, matrix products, shards(): jnp.dot(hidden, out_weight, preferred_element_type=jnp.float32)  16.8 us
  transfers between devices with their start and end apart: 8, of which 3 were waited for; matrix products, arithmetic and copies ran while one was open for 11% of the time, Pallas kernels for 0%

profile of v1, /device:TPU:0, one launch (start us, length us, event | category | flops | bytes accessed | tf_op | source)
XLA Modules:
  0.0 375.3 jit_solution(1062890051431968300)
XLA Ops:
  6.5 0.0 all-gather.2.cloned.1.call-start
  6.5 0.7 all-gather.2.cloned.1.call-update
  7.3 0.0 reduce-scatter.2.cloned.1.call-start
  7.3 0.0 copy-start.1
  7.3 129.9 %all-gather.2.cloned.1.call-done = bf16[512,8192]{1,0:T(8,128)(2,1)} async-done(((bf16[512,1024]{1,0:T(8,128)(2,1)}), bf16[512,8192]{1,0:T(8,128)(2,1)}) %all-gather.2.cloned.1.call-update) | async-done | bytes 8388624 | tf_op jit(solution)/shard_map/all_gather | solution.py:71
  137.2 4.6 %constant_dynamic-slice_fusion = bf16[512,4096]{1,0:T(8,128)(2,1)} fusion(bf16[512,8192]{1,0:T(8,128)(2,1)} %all-gather.2.cloned.1.call-done, s32[]{:T(128)S(6)} %select_n.6), kind=kLoop, calls=%fused_computation.25 | loop fusion | bytes 8388612 | tf_op jit(solution)/shard_map/dynamic_slice | solution.py:73
  141.8 0.0 collective-permute-start
  141.8 0.0 copy-done.1
  141.8 0.1 rev.3
  141.9 0.1 pad.6.clone
  142.0 0.1 maximum_bitcast_fusion.band_ref
  142.1 0.0 copy-start
  142.1 8.3 %fusion.4 = f32[512,1024]{1,0:T(8,128)S(1)} fusion(bf16[3,4096,1024]{2,1,0:T(8,128)(2,1)} %bitcast.27, bf16[512,8192]{1,0:T(8,128)(2,1)} %all-gather.2.cloned.1.call-done, s32[]{:T(128)S(6)} %select_n.7), kind=kOutput, calls=%fused_computation.8 | convolution fusion | flops 4294967296 | bytes 14680068 | tf_op jit(solution)/shard_map/dot_general | solution.py:76
  150.4 0.0 copy-done
  150.4 7.1 %fusion.2 = f32[512,1024]{1,0:T(8,128)S(1)} fusion(bf16[3,4096,1024]{2,1,0:T(8,128)(2,1)} %bitcast.28, bf16[512,8192]{1,0:T(8,128)(2,1)S(1)} %copy-done, s32[]{:T(128)S(6)} %select_n.7), kind=kOutput, calls=%fused_computation.6 | convolution fusion | flops 4294967296 | bytes 14680068 | tf_op jit(solution)/shard_map/dot_general | solution.py:76
  157.6 0.0 collective-permute-done
  157.6 9.1 %fusion.9 = bf16[512,1024]{1,0:T(8,128)(2,1)S(1)} fusion(bf16[512,4096]{1,0:T(8,128)(2,1)} %collective-permute-done, bf16[3,4096,1024]{2,1,0:T(8,128)(2,1)} %bitcast.29), kind=kOutput, calls=%fused_computation.16 | convolution fusion | flops 4295491584 | bytes 13631488 | tf_op jit(solution)/shard_map/dot_general | solution.py:76
  166.7 0.6 collective-permute-start.4
  167.3 9.1 %fusion.10 = bf16[512,1024]{1,0:T(8,128)(2,1)S(1)} fusion(bf16[512,4096]{1,0:T(8,128)(2,1)} %collective-permute-done, bf16[3,4096,1024]{2,1,0:T(8,128)(2,1)} %bitcast.30), kind=kOutput, calls=%fused_computation.17 | convolution fusion | flops 4295491584 | bytes 13631488 | tf_op jit(solution)/shard_map/dot_general | solution.py:76
  176.4 0.1 collective-permute-start.2
  176.5 9.1 %fusion.11 = bf16[512,1024]{1,0:T(8,128)(2,1)S(1)} fusion(bf16[512,4096]{1,0:T(8,128)(2,1)} %collective-permute-done, bf16[3,4096,1024]{2,1,0:T(8,128)(2,1)} %bitcast.31), kind=kOutput, calls=%fused_computation.18 | convolution fusion | flops 4295491584 | bytes 13631488 | tf_op jit(solution)/shard_map/dot_general | solution.py:76
  185.7 0.6 collective-permute-start.1
  186.2 6.9 %fusion = f32[512,1024]{1,0:T(8,128)S(1)} fusion(bf16[3,4096,1024]{2,1,0:T(8,128)(2,1)} %bitcast.32, bf16[512,8192]{1,0:T(8,128)(2,1)S(1)} %copy-done, s32[]{:T(128)S(6)} %select_n.7), kind=kOutput, calls=%fused_computation.4 | convolution fusion | flops 4294967296 | bytes 14680068 | tf_op jit(solution)/shard_map/dot_general | solution.py:76
  193.2 0.0 collective-permute-done.4
  193.2 0.4 add_convert_fusion
  193.6 1.9 collective-permute-start.5
  195.5 0.0 collective-permute-done.2
  195.6 0.4 add_convert_fusion.1
  196.0 1.5 collective-permute-start.3
  197.5 0.0 collective-permute-done.1
  197.5 0.4 add_convert_fusion.2.q_ref
  197.9 0.0 collective-permute-done.5
  197.9 0.1 pad_maximum_fusion.1.v_ref
  198.0 0.4 collective-permute-done.3
  198.4 0.1 pad_maximum_fusion.k_ref
  198.5 5.4 %shard_map.46 = bf16[512,1024]{1,0:T(8,128)(2,1)S(1)} custom-call(f32[8,8,256]{2,1,0:T(8,128)S(1)} %maximum_bitcast_fusion.band_ref, bf16[512,1024]{1,0:T(8,128)(2,1)S(1)} %add_convert_fusion.2.q_ref, bf16[640,1024]{1,0:T(8,128)(2,1)S(1)} %pad_maximum_fusion.k_ref, bf16[640,1024]{1,0:T(8,128)(2,1)S(1)} %pad_maximum_fusion.1.v_ref), custom_call_target="tpu_custom_call" | custom-call | tf_op jit(solution)/shard_map/pallas_call | solution.py:45
  203.9 16.8 %convolution_convert_fusion = bf16[512,8192]{1,0:T(8,128)(2,1)} fusion(bf16[512,1024]{1,0:T(8,128)(2,1)S(1)} %shard_map.46, bf16[1024,8192]{1,0:T(8,128)(2,1)} %param.7), kind=kOutput, calls=%fused_computation | convolution fusion | flops 8594128896 | bytes 26214400 | tf_op jit(solution)/shard_map/dot_general | solution.py:86
  220.7 0.0 reduce-scatter.2.cloned.1.call-update
  220.8 147.7 %reduce-scatter.2.cloned.1.call-done = bf16[512,1024]{1,0:T(8,128)(2,1)} async-done(((bf16[512,8192]{1,0:T(8,128)(2,1)}), bf16[512,1024]{1,0:T(8,128)(2,1)}) %reduce-scatter.2.cloned.1.call-update) | async-done | bytes 1048592 | tf_op jit(solution)/shard_map/reduce_scatter | solution.py:87
  (4 shorter events, 0.0 us)
Async XLA Ops:
  6.5 130.7 %all-gather.2.cloned.1.call-start = ((), (), s32[]{:S(2)}) async-start(), calls=%async_computation.1 | async-start | bytes 9437184 | tf_op jit(solution)/shard_map/all_gather | solution.py:71
  7.3 361.2 %reduce-scatter.2.cloned.1.call-start = ((), (), s32[]{:S(2)}) async-start(), calls=%async_computation.2 | async-start | bytes 9437184 | tf_op jit(solution)/shard_map/reduce_scatter | solution.py:87
  7.3 134.5 %copy-start.1 = (f32[64,128]{1,0:T(8,128)S(1)}, f32[64,128]{1,0:T(8,128)}, u32[]{:S(2)}) copy-start(f32[64,128]{1,0:T(8,128)} %param.6) | copy-start | bytes 98308
  141.8 15.7 %collective-permute-start = (bf16[512,4096]{1,0:T(8,128)(2,1)}, bf16[512,4096]{1,0:T(8,128)(2,1)}, u32[]{:S(2)}, u32[]{:S(2)}) collective-permute-start(bf16[512,4096]{1,0:T(8,128)(2,1)} %constant_dynamic-slice_fusion), channel_id=1, source_target_pairs={{0,1},{1,0},{2,3},{3,2},{4,5},{5,4},{6,7},{7,6},{8,9},{9,8},{10,11... | collective-permute-start | bytes 12582920 | tf_op jit(solution)/shard_map/ppermute | solution.py:61
  142.1 8.3 %copy-start = (bf16[512,8192]{1,0:T(8,128)(2,1)S(1)}, bf16[512,8192]{1,0:T(8,128)(2,1)}, u32[]{:S(2)}) copy-start(bf16[512,8192]{1,0:T(8,128)(2,1)} %all-gather.2.cloned.1.call-done) | copy-start | bytes 25165828
  166.7 26.5 %collective-permute-start.4 = (bf16[512,1024]{1,0:T(8,128)(2,1)S(1)}, bf16[512,1024]{1,0:T(8,128)(2,1)S(1)}, u32[]{:S(2)}, u32[]{:S(2)}) collective-permute-start(bf16[512,1024]{1,0:T(8,128)(2,1)S(1)} %fusion.9), channel_id=1, source_target_pairs={{0,1},{1,0},{2,3},{3,2},{4,5},{5,4},{6,7},{7,6},{8,9},{9,8},{10,11... | collective-permute-start | bytes 3145736 | tf_op jit(solution)/shard_map/ppermute | solution.py:61
  176.4 19.1 %collective-permute-start.2 = (bf16[512,1024]{1,0:T(8,128)(2,1)S(1)}, bf16[512,1024]{1,0:T(8,128)(2,1)S(1)}, u32[]{:S(2)}, u32[]{:S(2)}) collective-permute-start(bf16[512,1024]{1,0:T(8,128)(2,1)S(1)} %fusion.10), channel_id=1, source_target_pairs={{0,1},{1,0},{2,3},{3,2},{4,5},{5,4},{6,7},{7,6},{8,9},{9,8},{10,11... | collective-permute-start | bytes 3145736 | tf_op jit(solution)/shard_map/ppermute | solution.py:61
  185.7 11.8 %collective-permute-start.1 = (bf16[512,1024]{1,0:T(8,128)(2,1)S(1)}, bf16[512,1024]{1,0:T(8,128)(2,1)S(1)}, u32[]{:S(2)}, u32[]{:S(2)}) collective-permute-start(bf16[512,1024]{1,0:T(8,128)(2,1)S(1)} %fusion.11), channel_id=1, source_target_pairs={{0,1},{1,0},{2,3},{3,2},{4,5},{5,4},{6,7},{7,6},{8,9},{9,8},{10,11... | collective-permute-start | bytes 3145736 | tf_op jit(solution)/shard_map/ppermute | solution.py:61
  193.6 4.3 %collective-permute-start.5 = (bf16[128,1024]{1,0:T(8,128)(2,1)S(1)}, bf16[128,1024]{1,0:T(8,128)(2,1)S(1)}, u32[]{:S(2)}, u32[]{:S(2)}) collective-permute-start(bf16[128,1024]{1,0:T(8,128)(2,1)S(1)} %slice.27), channel_id=1, source_target_pairs={{0,1},{2,3},{4,5},{6,7},{8,9},{10,11},{12,13},{14,15},{16,17},{18,... | collective-permute-start | bytes 786440 | tf_op jit(solution)/shard_map/ppermute | solution.py:83
  196.0 2.4 collective-permute-start.3
Sparse Core Ops, SparseCore 0:
  9.5 127.6 all-gather.1
  220.9 147.5 reduce-scatter.1

commit v2 on v1

--- a/solution.py
+++ b/solution.py
@@ -68,25 +68,39 @@
     taps = filters.shape[1]
     me = lax.axis_index("tok")
     panel = jnp.transpose(in_weight, (1, 0, 2))
-    full = lax.all_gather(tokens, "feat", axis=1, tiled=True)
-    mine = lax.dynamic_slice_in_dim(full, me * depth, depth, 1)
-    theirs = swap(lax.dynamic_slice_in_dim(full, (1 - me) * depth, depth, 1))
+    cuts = 2
+    step = rows // cuts
 
     def project(x):
         return [jnp.dot(x, panel[s], preferred_element_type=jnp.float32) for s in range(3)]
 
-    away = [swap(p.astype(jnp.bfloat16)) for p in project(theirs)]
-    home = project(mine)
-    q, k, v = [(a.astype(jnp.float32) + b).astype(jnp.bfloat16) for a, b in zip(away, home)]
+    pieces = []
+    for c in range(cuts):
+        block = tokens[c * step : (c + 1) * step]
+        if c > 0:
+            block, full = lax.optimization_barrier((block, full))
+        full = lax.all_gather(block, "feat", axis=1, tiled=True)
+        theirs = swap(lax.dynamic_slice_in_dim(full, (1 - me) * depth, depth, 1))
+        home = project(lax.dynamic_slice_in_dim(full, me * depth, depth, 1))
+        away = [swap(p.astype(jnp.bfloat16)) for p in project(theirs)]
+        pieces.append([(a.astype(jnp.float32) + b).astype(jnp.bfloat16) for a, b in zip(away, home)])
+    q, k, v = [jnp.concatenate(x, axis=0) for x in zip(*pieces)]
 
     def extend(x):
         return jnp.concatenate([lax.ppermute(x[rows - taps :], "tok", [(0, 1)]), x], axis=0)
 
     hidden = convolve(filters, q, extend(k), extend(v))
-    partial_rows = jnp.dot(hidden, out_weight, preferred_element_type=jnp.float32)
-    return lax.psum_scatter(
-        partial_rows.astype(jnp.bfloat16), "feat", scatter_dimension=1, tiled=True
-    )
+    results = []
+    for c in range(cuts):
+        partial_rows = jnp.dot(
+            hidden[c * step : (c + 1) * step], out_weight, preferred_element_type=jnp.float32
+        )
+        results.append(
+            lax.psum_scatter(
+                partial_rows.astype(jnp.bfloat16), "feat", scatter_dimension=1, tiled=True
+            )
+        )
+    return jnp.concatenate(results, axis=0)
 
 
 def solution(mesh):

time: 376 us -> 407 us (1.082)
  matrix products: 66.6 us -> 91.5 us
    all_gather x1 -> x2, waiting for transfers between devices: 130 us -> 109 us  [shards(): full = lax.all_gather(block, 'feat', axis=1, tiled=True)]
    reduce_scatter x1 -> x2, waiting for transfers between devices: 148 us -> 167 us  [shards(): lax.psum_scatter(partial_rows.astype(jnp.bfloat16), 'feat', scatter_dimen...]
    dot_general x6 -> x12, matrix products: 49.8 us -> 67.6 us  [project(): jnp.dot(x, panel[s], preferred_element_type=jnp.float32)]
    dot_general x1 -> x2, matrix products: 16.8 us -> 23.9 us  [shards(): jnp.dot(hidden[c * step:(c + 1) * step], out_weight, preferred_element_ty...]
  transfers between devices with their start and end apart: 8 -> 14, of which waited for: 3 -> 6; matrix products, arithmetic and copies ran while one was open for 11% -> 19% of each run, Pallas kernels for 0% -> 0%
where the time goes in v2:
time: 407 us; the launch traced here: 406 us
  waiting for transfers between devices  278 us (68%)
  matrix products  91.5 us (22%)
  between operations  13.6 us (3%)
  local copies, waits for them, and re-layouts  8.67 us (2%)
  starting transfers between devices  5.67 us (1%)
  Pallas kernels  5.4 us (1%)
    reduce_scatter x2, waiting for transfers between devices, shards(): lax.psum_scatter(partial_rows.astype(jnp.bfloat16), 'feat', scatter_dimen...  167 us
    all_gather x2, waiting for transfers between devices, shards(): full = lax.all_gather(block, 'feat', axis=1, tiled=True)  109 us
    dot_general x12, matrix products, project(): jnp.dot(x, panel[s], preferred_element_type=jnp.float32)  67.6 us
    dot_general x2, matrix products, shards(): jnp.dot(hidden[c * step:(c + 1) * step], out_weight, preferred_element_ty...  23.9 us
  transfers between devices with their start and end apart: 14, of which 6 were waited for; matrix products, arithmetic and copies ran while one was open for 19% of the time, Pallas kernels for 0%

profile of v2, /device:TPU:0, one launch (start us, length us, event | category | flops | bytes accessed | tf_op | source)
XLA Modules:
  0.0 405.9 jit_solution(1146972876971024350)
XLA Ops:
  6.5 2.3 fusion.32
  8.8 0.0 all-gather.3.cloned.1.call-update
  8.9 0.0 all-gather.5.cloned.1.call-start
  8.9 76.7 %all-gather.3.cloned.1.call-done = bf16[256,8192]{1,0:T(8,128)(2,1)} async-done(((bf16[256,1024]{1,0:T(8,128)(2,1)}), bf16[256,8192]{1,0:T(8,128)(2,1)}) %all-gather.3.cloned.1.call-update) | async-done | bytes 4194320 | tf_op jit(solution)/shard_map/all_gather | solution.py:82
  85.7 0.0 all-gather.5.cloned.1.call-update
  85.7 0.0 reduce-scatter.5.cloned.1.call-start
  85.7 0.1 pad.12.clone
  85.8 0.8 rev.3
  86.7 0.1 maximum_bitcast_fusion.band_ref
  86.7 2.0 constant_dynamic-slice_fusion.1
  88.7 0.1 collective-permute-start
  88.8 0.7 copy-done.1
  89.5 5.8 %fusion.4 = f32[256,1024]{1,0:T(8,128)S(1)} fusion(bf16[3,4096,1024]{2,1,0:T(8,128)(2,1)} %bitcast.42, bf16[256,8192]{1,0:T(8,128)(2,1)S(1)} %copy-done.1, s32[]{:T(128)S(6)} %select_n.9), kind=kOutput, calls=%fused_computation.9 | convolution fusion | flops 2147483648 | bytes 11534340 | tf_op jit(solution)/shard_map/dot_general | solution.py:75
  95.3 5.8 %fusion.8 = f32[256,1024]{1,0:T(8,128)S(1)} fusion(bf16[3,4096,1024]{2,1,0:T(8,128)(2,1)} %bitcast.43, bf16[256,8192]{1,0:T(8,128)(2,1)S(1)} %copy-done.1, s32[]{:T(128)S(6)} %select_n.9), kind=kOutput, calls=%fused_computation.13 | convolution fusion | flops 2147483648 | bytes 11534340 | tf_op jit(solution)/shard_map/dot_general | solution.py:75
  101.1 5.8 %fusion.2 = f32[256,1024]{1,0:T(8,128)S(1)} fusion(bf16[3,4096,1024]{2,1,0:T(8,128)(2,1)} %bitcast.44, bf16[256,8192]{1,0:T(8,128)(2,1)S(1)} %copy-done.1, s32[]{:T(128)S(6)} %select_n.9), kind=kOutput, calls=%fused_computation.7 | convolution fusion | flops 2147483648 | bytes 11534340 | tf_op jit(solution)/shard_map/dot_general | solution.py:75
  106.9 0.0 collective-permute-done
  106.9 5.8 %fusion.22 = bf16[256,1024]{1,0:T(8,128)(2,1)S(1)} fusion(bf16[256,4096]{1,0:T(8,128)(2,1)S(1)} %collective-permute-done, bf16[3,4096,1024]{2,1,0:T(8,128)(2,1)} %bitcast.45), kind=kOutput, calls=%fused_computation.29 | convolution fusion | flops 2147745792 | bytes 11010048 | tf_op jit(solution)/shard_map/dot_general | solution.py:75
  112.7 0.1 collective-permute-start.1
  112.8 5.8 %fusion.21 = bf16[256,1024]{1,0:T(8,128)(2,1)S(1)} fusion(bf16[256,4096]{1,0:T(8,128)(2,1)S(1)} %collective-permute-done, bf16[3,4096,1024]{2,1,0:T(8,128)(2,1)} %bitcast.46), kind=kOutput, calls=%fused_computation.28 | convolution fusion | flops 2147745792 | bytes 11010048 | tf_op jit(solution)/shard_map/dot_general | solution.py:75
  118.6 0.6 collective-permute-start.6
  119.2 6.2 %fusion.19 = bf16[256,1024]{1,0:T(8,128)(2,1)S(1)} fusion(bf16[256,4096]{1,0:T(8,128)(2,1)S(1)} %collective-permute-done, bf16[3,4096,1024]{2,1,0:T(8,128)(2,1)} %bitcast.47), kind=kOutput, calls=%fused_computation.26 | convolution fusion | flops 2147745792 | bytes 11010048 | tf_op jit(solution)/shard_map/dot_general | solution.py:75
  125.4 0.2 collective-permute-start.9
  125.6 0.2 add_convert_fusion.5
  125.7 0.0 collective-permute-done.6
  125.7 0.2 add_convert_fusion.2
  125.9 1.5 collective-permute-done.9
  127.4 0.2 add_convert_fusion
  127.6 32.0 %all-gather.5.cloned.1.call-done = bf16[256,8192]{1,0:T(8,128)(2,1)} async-done(((bf16[256,1024]{1,0:T(8,128)(2,1)}), bf16[256,8192]{1,0:T(8,128)(2,1)}) %all-gather.5.cloned.1.call-update) | async-done | bytes 4194320 | tf_op jit(solution)/shard_map/all_gather | solution.py:82
  159.5 1.9 constant_dynamic-slice_fusion
  161.5 0.1 collective-permute-start.2
  161.6 0.8 copy-done
  162.3 6.0 %fusion.6 = f32[256,1024]{1,0:T(8,128)S(1)} fusion(bf16[3,4096,1024]{2,1,0:T(8,128)(2,1)} %bitcast.48, bf16[256,8192]{1,0:T(8,128)(2,1)S(1)} %copy-done, s32[]{:T(128)S(6)} %select_n.9), kind=kOutput, calls=%fused_computation.11 | convolution fusion | flops 2147483648 | bytes 11534340 | tf_op jit(solution)/shard_map/dot_general | solution.py:75
  168.3 0.0 slice-start
  168.3 5.9 %fusion.10 = f32[256,1024]{1,0:T(8,128)S(1)} fusion(bf16[3,4096,1024]{2,1,0:T(8,128)(2,1)} %bitcast.49, bf16[256,8192]{1,0:T(8,128)(2,1)S(1)} %copy-done, s32[]{:T(128)S(6)} %select_n.9), kind=kOutput, calls=%fused_computation.15 | convolution fusion | flops 2147483648 | bytes 11534340 | tf_op jit(solution)/shard_map/dot_general | solution.py:75
  174.3 0.0 slice-start.2
  174.3 5.9 %fusion = f32[256,1024]{1,0:T(8,128)S(1)} fusion(bf16[3,4096,1024]{2,1,0:T(8,128)(2,1)} %bitcast.50, bf16[256,8192]{1,0:T(8,128)(2,1)S(1)} %copy-done, s32[]{:T(128)S(6)} %select_n.9), kind=kOutput, calls=%fused_computation.5 | convolution fusion | flops 2147483648 | bytes 11534340 | tf_op jit(solution)/shard_map/dot_general | solution.py:75
  180.3 0.0 slice-start.4
  180.3 0.0 collective-permute-done.2
  180.3 6.5 %fusion.20 = bf16[256,1024]{1,0:T(8,128)(2,1)S(1)} fusion(bf16[256,4096]{1,0:T(8,128)(2,1)} %collective-permute-done.2, bf16[3,4096,1024]{2,1,0:T(8,128)(2,1)} %bitcast.51), kind=kOutput, calls=%fused_computation.27 | convolution fusion | flops 2147745792 | bytes 11010048 | tf_op jit(solution)/shard_map/dot_general | solution.py:75
  186.8 0.1 collective-permute-start.4
  186.9 4.0 fusion.18
  190.9 0.5 collective-permute-start.7
  191.5 4.0 fusion.23
  195.5 0.1 collective-permute-start.3
  195.6 0.0 collective-permute-done.4
  195.6 0.1 add_convert_fusion.3
  195.8 2.4 collective-permute-start.5
  198.2 0.2 add_convert_fusion.1
  198.4 1.5 collective-permute-start.8
  199.9 0.2 add_convert_fusion.4
  200.1 0.1 pad_maximum_fusion.2.q_ref
  200.2 0.0 collective-permute-done.5
  200.2 0.1 pad_maximum_fusion.k_ref
  200.3 0.5 collective-permute-done.8
  200.8 0.1 pad_maximum_fusion.1.v_ref
  200.9 5.4 %shard_map.46 = bf16[512,1024]{1,0:T(8,128)(2,1)S(1)} custom-call(f32[8,8,256]{2,1,0:T(8,128)S(1)} %maximum_bitcast_fusion.band_ref, bf16[512,1024]{1,0:T(8,128)(2,1)S(1)} %pad_maximum_fusion.2.q_ref, bf16[640,1024]{1,0:T(8,128)(2,1)S(1)} %pad_maximum_fusion.k_ref, bf16[640,1024]{1,0:T(8,128)(2,1)S(1)} %pad_maximum_fusion.1.v_ref), custom_call_target="tpu_custom_call" | custom-call | tf_op jit(solution)/shard_map/pallas_call | solution.py:45
  206.3 11.8 %convolution_convert_fusion = bf16[256,8192]{1,0:T(8,128)(2,1)} fusion(bf16[1024,8192]{1,0:T(8,128)(2,1)} %param.7, bf16[512,1024]{1,0:T(8,128)(2,1)S(1)} %shard_map.46), kind=kOutput, calls=%fused_computation | convolution fusion | flops 4297064448 | bytes 21495808 | tf_op jit(solution)/shard_map/dot_general | solution.py:95
  218.2 0.0 reduce-scatter.5.cloned.1.call-update
  218.2 0.0 reduce-scatter.3.cloned.1.call-start
  218.2 12.0 %convolution_convert_fusion.1 = bf16[256,8192]{1,0:T(8,128)(2,1)} fusion(bf16[1024,8192]{1,0:T(8,128)(2,1)} %param.7, bf16[512,1024]{1,0:T(8,128)(2,1)S(1)} %shard_map.46), kind=kOutput, calls=%fused_computation.1 | convolution fusion | flops 4297064448 | bytes 21495808 | tf_op jit(solution)/shard_map/dot_general | solution.py:95
  230.3 0.0 reduce-scatter.3.cloned.1.call-update
  230.3 74.8 %reduce-scatter.5.cloned.1.call-done = bf16[256,1024]{1,0:T(8,128)(2,1)} async-done(((bf16[256,8192]{1,0:T(8,128)(2,1)}), bf16[256,1024]{1,0:T(8,128)(2,1)}) %reduce-scatter.5.cloned.1.call-update) | async-done | bytes 524304 | tf_op jit(solution)/shard_map/reduce_scatter | solution.py:99
  305.1 92.0 %reduce-scatter.3.cloned.1.call-done = bf16[256,1024]{1,0:T(8,128)(2,1)} async-done(((bf16[256,8192]{1,0:T(8,128)(2,1)}), bf16[256,1024]{1,0:T(8,128)(2,1)}) %reduce-scatter.3.cloned.1.call-update) | async-done | bytes 524304 | tf_op jit(solution)/shard_map/reduce_scatter | solution.py:99
  397.1 2.2 pad_maximum_fusion.3
  (20 shorter events, 0.1 us)
Async XLA Ops:
  6.5 79.1 %all-gather.3.cloned.1.call-start = ((), (), s32[]{:S(2)}) async-start(), calls=%async_computation.2 | async-start | bytes 4718592 | tf_op jit(solution)/shard_map/all_gather | solution.py:82
  8.9 150.6 %all-gather.5.cloned.1.call-start = ((), (), s32[]{:S(2)}) async-start(), calls=%async_computation.3 | async-start | bytes 4718592 | tf_op jit(solution)/shard_map/all_gather | solution.py:82
  85.7 219.4 %reduce-scatter.5.cloned.1.call-start = ((), (), s32[]{:S(2)}) async-start(), calls=%async_computation.5 | async-start | bytes 4718592 | tf_op jit(solution)/shard_map/reduce_scatter | solution.py:99
  86.7 2.8 copy-start.1
  88.7 18.2 %collective-permute-start = (bf16[256,4096]{1,0:T(8,128)(2,1)S(1)}, bf16[256,4096]{1,0:T(8,128)(2,1)S(1)}, u32[]{:S(2)}, u32[]{:S(2)}) collective-permute-start(bf16[256,4096]{1,0:T(8,128)(2,1)S(1)} %constant_dynamic-slice_fusion.1), channel_id=1, source_target_pairs={{0,1},{1,0},{2,3},{3,2},{4,5},{5,4},{6,7},{7,6},{8,9},{9,8},{10,11... | collective-permute-start | bytes 6291464 | tf_op jit(solution)/shard_map/ppermute | solution.py:61
  112.7 12.8 %collective-permute-start.1 = (bf16[256,1024]{1,0:T(8,128)(2,1)S(1)}, bf16[256,1024]{1,0:T(8,128)(2,1)S(1)}, u32[]{:S(2)}, u32[]{:S(2)}) collective-permute-start(bf16[256,1024]{1,0:T(8,128)(2,1)S(1)} %fusion.22), channel_id=1, source_target_pairs={{0,1},{1,0},{2,3},{3,2},{4,5},{5,4},{6,7},{7,6},{8,9},{9,8},{10,11... | collective-permute-start | bytes 1572872 | tf_op jit(solution)/shard_map/ppermute | solution.py:61
  118.6 7.1 %collective-permute-start.6 = (bf16[256,1024]{1,0:T(8,128)(2,1)S(1)}, bf16[256,1024]{1,0:T(8,128)(2,1)S(1)}, u32[]{:S(2)}, u32[]{:S(2)}) collective-permute-start(bf16[256,1024]{1,0:T(8,128)(2,1)S(1)} %fusion.21), channel_id=1, source_target_pairs={{0,1},{1,0},{2,3},{3,2},{4,5},{5,4},{6,7},{7,6},{8,9},{9,8},{10,11... | collective-permute-start | bytes 1572872 | tf_op jit(solution)/shard_map/ppermute | solution.py:61
  125.4 2.0 collective-permute-start.9
  159.5 2.8 copy-start
  161.5 18.8 %collective-permute-start.2 = (bf16[256,4096]{1,0:T(8,128)(2,1)S(1)}, bf16[256,4096]{1,0:T(8,128)(2,1)}, u32[]{:S(2)}, u32[]{:S(2)}) collective-permute-start(bf16[256,4096]{1,0:T(8,128)(2,1)S(1)} %constant_dynamic-slice_fusion), channel_id=1, source_target_pairs={{0,1},{1,0},{2,3},{3,2},{4,5},{5,4},{6,7},{7,6},{8,9},{9,8},{10,11... | collective-permute-start | bytes 6291464 | tf_op jit(solution)/shard_map/ppermute | solution.py:61
  168.3 18.6 %slice-start = ((s8[25165824]{0:T(1024)(128)(4,1)}), s8[4194304]{0:T(1024)(128)(4,1)S(1)}, s32[]{:S(2)}) async-start(s8[25165824]{0:T(1024)(128)(4,1)} %bitcast.52), calls=%async_computation.6 | async-start | bytes 8388608
  168.3 18.6 %slice-start.1 = ((s8[25165824]{0:T(1024)(128)(4,1)}), s8[4194304]{0:T(1024)(128)(4,1)S(1)}, s32[]{:S(2)}) async-start(s8[25165824]{0:T(1024)(128)(4,1)} %bitcast.52), calls=%async_computation.7 | async-start | bytes 8388608
  174.3 12.6 %slice-start.2 = ((s8[25165824]{0:T(1024)(128)(4,1)}), s8[4194304]{0:T(1024)(128)(4,1)S(1)}, s32[]{:S(2)}) async-start(s8[25165824]{0:T(1024)(128)(4,1)} %bitcast.52), calls=%async_computation.8 | async-start | bytes 8388608
  174.3 12.6 %slice-start.3 = ((s8[25165824]{0:T(1024)(128)(4,1)}), s8[4194304]{0:T(1024)(128)(4,1)S(1)}, s32[]{:S(2)}) async-start(s8[25165824]{0:T(1024)(128)(4,1)} %bitcast.52), calls=%async_computation.9 | async-start | bytes 8388608
  180.3 6.7 %slice-start.4 = ((s8[25165824]{0:T(1024)(128)(4,1)}), s8[4194304]{0:T(1024)(128)(4,1)S(1)}, s32[]{:S(2)}) async-start(s8[25165824]{0:T(1024)(128)(4,1)} %bitcast.52), calls=%async_computation.10 | async-start | bytes 8388608
  180.3 6.6 %slice-start.5 = ((s8[25165824]{0:T(1024)(128)(4,1)}), s8[4194304]{0:T(1024)(128)(4,1)S(1)}, s32[]{:S(2)}) async-start(s8[25165824]{0:T(1024)(128)(4,1)} %bitcast.52), calls=%async_computation.11 | async-start | bytes 8388608
  186.8 8.8 %collective-permute-start.4 = (bf16[256,1024]{1,0:T(8,128)(2,1)S(1)}, bf16[256,1024]{1,0:T(8,128)(2,1)S(1)}, u32[]{:S(2)}, u32[]{:S(2)}) collective-permute-start(bf16[256,1024]{1,0:T(8,128)(2,1)S(1)} %fusion.20), channel_id=1, source_target_pairs={{0,1},{1,0},{2,3},{3,2},{4,5},{5,4},{6,7},{7,6},{8,9},{9,8},{10,11... | collective-permute-start | bytes 1572872 | tf_op jit(solution)/shard_map/ppermute | solution.py:61
  190.9 7.2 %collective-permute-start.7 = (bf16[256,1024]{1,0:T(8,128)(2,1)S(1)}, bf16[256,1024]{1,0:T(8,128)(2,1)S(1)}, u32[]{:S(2)}, u32[]{:S(2)}) collective-permute-start(bf16[256,1024]{1,0:T(8,128)(2,1)S(1)} %fusion.18), channel_id=1, source_target_pairs={{0,1},{1,0},{2,3},{3,2},{4,5},{5,4},{6,7},{7,6},{8,9},{9,8},{10,11... | collective-permute-start | bytes 1572872 | tf_op jit(solution)/shard_map/ppermute | solution.py:61
  195.5 4.4 %collective-permute-start.3 = (bf16[256,1024]{1,0:T(8,128)(2,1)S(1)}, bf16[256,1024]{1,0:T(8,128)(2,1)S(1)}, u32[]{:S(2)}, u32[]{:S(2)}) collective-permute-start(bf16[256,1024]{1,0:T(8,128)(2,1)S(1)} %fusion.23), channel_id=1, source_target_pairs={{0,1},{1,0},{2,3},{3,2},{4,5},{5,4},{6,7},{7,6},{8,9},{9,8},{10,11... | collective-permute-start | bytes 1572872 | tf_op jit(solution)/shard_map/ppermute | solution.py:61
  195.8 4.4 %collective-permute-start.5 = (bf16[128,1024]{1,0:T(8,128)(2,1)S(1)}, bf16[128,1024]{1,0:T(8,128)(2,1)S(1)}, u32[]{:S(2)}, u32[]{:S(2)}) collective-permute-start(bf16[128,1024]{1,0:T(8,128)(2,1)S(1)} %slice.47), channel_id=1, source_target_pairs={{0,1},{2,3},{4,5},{6,7},{8,9},{10,11},{12,13},{14,15},{16,17},{18,... | collective-permute-start | bytes 786440 | tf_op jit(solution)/shard_map/ppermute | solution.py:90
  198.4 2.4 collective-permute-start.8
  218.2 178.9 %reduce-scatter.3.cloned.1.call-start = ((), (), s32[]{:S(2)}) async-start(), calls=%async_computation.4 | async-start | bytes 4718592 | tf_op jit(solution)/shard_map/reduce_scatter | solution.py:99
Sparse Core Ops, SparseCore 0:
  9.5 76.0 all-gather.2
  87.8 71.6 all-gather.4
  218.3 86.7 reduce-scatter.4
  309.0 88.0 reduce-scatter.2
